TPU v7x, 128 devices: a whole 4x4x4 slice. The times are simulated.
128 devices in a mesh: grp: 4 (over x), blk: 32 (over y, z, core).
Axes of the slice: x: 4, y: 4, z: 4, core: 2. Of those that a mesh axis runs over, the one named last changes fastest.
Arguments:
- t2_tiles: bfloat16 [1024, 64, 2304], P(('grp', 'blk')), may hold values from -6 to 6
- t2_shape: int32 [1024, 1], P(('grp', 'blk')), may hold values 0 or 1
- owners: int32 [1024, 1], P(('grp', 'blk')), may hold values from 0 to 3; in each aligned block of 8 rows (0 to 7, 8 to 15, ...) at most 4 rows name the same one
- integrals: bfloat16 [2304, 2304], P('blk'), may hold values from -0.125 to 0.125
Outputs:
- residual: bfloat16 [2048, 64, 2304], P(('grp', 'blk'))
Inputs may be any that keep to these rules, and one draw needn't show every extreme that they name: `owners`: among the 8 tiles of one device, no group is named more than 4 times, a bound that some block reaches.
All inputs are finite; a program needn't handle non-finite values. No bound on the sum of `t2_shape` on one device may be relied on, other than what follows from the above.
Results may differ from a plain program's by a relative error of at most 0.001.
Values may be sent and summed in bfloat16 or wider, within the bound.
No kernel may reach another device: no remote copies, remote signals or barrier semaphores. Data moves between devices by JAX's collectives and lax.ppermute only.
A program may use at most 64 MiB of HBM per device.

v0:
```python
import functools

import jax
import jax.numpy as jnp
from jax import lax
from jax.experimental import pallas as pl
from jax.experimental.pallas import tpu as pltpu
from jax.sharding import PartitionSpec as P

Y = 4
CAP = 4
MARK = 16
ANY = pl.BlockSpec(memory_space=pl.ANY)
SMEM = pl.BlockSpec(memory_space=pltpu.SMEM)
VMEM = pl.BlockSpec(memory_space=pltpu.VMEM)
BF16 = jnp.bfloat16


def pack_kernel(owners_hbm, shape_hbm, t2, code, out, owners, shape, tiles, mark, sem_s, sem_i, sem_o, sem_m):
    small = [pltpu.make_async_copy(owners_hbm, owners, sem_s.at[0]), pltpu.make_async_copy(shape_hbm, shape, sem_s.at[1])]
    for load in small:
        load.start()
    loads = [pltpu.make_async_copy(t2.at[t], tiles.at[t], sem_i.at[t]) for t in range(8)]
    for load in loads:
        load.start()
    mark[...] = jnp.full(mark.shape, jnp.nan, mark.dtype)
    for load in small:
        load.wait()
    taken = jnp.int32(0)
    for t in range(8):
        rank = 0
        for e in range(t):
            rank = rank + (owners[e] == owners[t]).astype(jnp.int32)
        live = (shape[t] > 0).astype(jnp.int32)
        code[t] = owners[t] + 4 * rank + 16 * live
        taken = taken | lax.shift_left(live, owners[t] * CAP + rank)

    def marks(do):
        for s in range(16):

            @pl.when(lax.bitwise_and(lax.shift_right_logical(taken, s), 1) == 0)
            def _():
                do(pltpu.make_async_copy(mark, out.at[s // CAP, s % CAP, pl.ds(0, MARK), pl.ds(0, 128)], sem_m.at[s]))

    def moves(do):
        for t in range(8):

            @pl.when(code[t] >= 16)
            def _():
                place = out.at[lax.bitwise_and(code[t], 3), lax.bitwise_and(lax.shift_right_logical(code[t], 2), 3)]
                do(loads[t], pltpu.make_async_copy(tiles.at[t], place, sem_o.at[t]))

            if do is start:

                @pl.when(code[t] < 16)
                def _():
                    loads[t].wait()

    def start(load, move):
        load.wait()
        move.start()

    marks(lambda c: c.start())
    moves(start)
    marks(lambda c: c.wait())
    moves(lambda load, move: move.wait())


def pack(owners, shape, t2):
    return pl.pallas_call(
        pack_kernel,
        out_shape=(jax.ShapeDtypeStruct((8,), jnp.int32), jax.ShapeDtypeStruct((4, CAP) + t2.shape[1:], t2.dtype)),
        in_specs=[ANY, ANY, ANY],
        out_specs=(SMEM, ANY),
        scratch_shapes=[
            pltpu.SMEM((8,), jnp.int32),
            pltpu.SMEM((8,), jnp.int32),
            pltpu.VMEM(t2.shape, t2.dtype),
            pltpu.VMEM((MARK, 128), t2.dtype),
            pltpu.SemaphoreType.DMA((2,)),
            pltpu.SemaphoreType.DMA((8,)),
            pltpu.SemaphoreType.DMA((8,)),
            pltpu.SemaphoreType.DMA((16,)),
        ],
        compiler_params=pltpu.CompilerParams(vmem_limit_bytes=56 << 20),
        cost_estimate=pl.CostEstimate(flops=0, bytes_accessed=4_700_000, transcendentals=0),
    )(owners, shape, t2)


def chips_of(y, z, c):
    a, b = jnp.where(c == 0, y, z), jnp.where(c == 0, z, y)

    def chip(da, db):
        aa, bb = lax.bitwise_and(a + da, 3), lax.bitwise_and(b + db, 3)
        return jnp.where(c == 0, aa * Y + bb, bb * Y + aa)

    near = lambda db: [chip(0, db), chip(-1, db)]
    wide = lambda db: [chip(1, db), chip(2, db)]
    return near(0) + wide(0) + near(-1) + wide(1) + wide(-1) + near(1) + near(2) + wide(2)


def product_kernel(code, local, arrived, *refs):
    mine, sibling, refs = refs[:8], refs[8:16], refs[16:]
    out, rows, matrix, result, zero, source, order, sem_t, sem_i, sem_o, sem_z = refs
    g, b = lax.axis_index("grp"), lax.axis_index("blk")
    y, z, c = lax.shift_right_logical(b, 3), lax.bitwise_and(lax.shift_right_logical(b, 1), 3), lax.bitwise_and(b, 1)
    half = matrix.shape[1] // 2
    height = mine[0].shape[1]
    width = matrix.shape[0]
    step, occ = 256, rows.shape[1]

    for s in range(16):
        source[s] = -1
    for t in range(8):
        rank = lax.bitwise_and(lax.shift_right_logical(code[t], 2), 3)

        @pl.when((code[t] >= 16) & (lax.bitwise_and(code[t], 3) == g))
        def _():
            source[g * CAP + rank] = t

    for s in range(16):
        own = g == s // CAP

        @pl.when(own)
        def _():
            pltpu.make_async_copy(local.at[jnp.maximum(source[s], 0)], rows.at[s], sem_t.at[s]).start()

        @pl.when(jnp.logical_not(own))
        def _():
            pltpu.make_async_copy(arrived.at[s // CAP, s % CAP], rows.at[s], sem_t.at[s]).start()

    copies = []
    for side, buffers in enumerate((mine, sibling)):
        core = c if side == 0 else 1 - c
        pieces = [buffer.at[k] for buffer in buffers for k in range(2)]
        for n, (piece, chip) in enumerate(zip(pieces, chips_of(y, z, core), strict=True)):
            to = matrix.at[pl.ds(pl.multiple_of(chip * height, height), height), pl.ds(pl.multiple_of(core * half, 128), half)]
            copies.append(pltpu.make_async_copy(piece, to, sem_i.at[side, n]))
    for copy in copies:
        copy.start()

    zero[...] = jnp.zeros_like(zero)
    for s in range(16):
        pltpu.make_async_copy(local.at[0], rows.at[s], sem_t.at[s]).wait()
    count = jnp.int32(0)
    for s in range(16):
        found = jnp.max(jnp.where(jnp.isnan(rows[s, :MARK, :128].astype(jnp.float32)), 0.0, 1.0)) > 0.5
        taken = ((g == s // CAP) & (source[s] >= 0)) | ((g != s // CAP) & found)
        order[s] = 0

        @pl.when(taken)
        def _():
            order[count] = s

        @pl.when(jnp.logical_not(taken))
        def _():
            pltpu.make_async_copy(zero, out.at[s], sem_z.at[s]).start()

        source[s] = taken.astype(jnp.int32)
        count = count + taken.astype(jnp.int32)

    for copy in copies:
        copy.wait()

    split = (width // step // 2 + 1) * step
    cuts = ((0, split), (split, width - split))

    def one_pass(group, start, end):
        tile = lambda j: order[jnp.minimum(start + j, 15)]
        left = jnp.concatenate([rows[tile(j)] for j in range(group)], axis=0)
        for n in range(width // step):
            right = matrix[n * step : (n + 1) * step, :]
            acc = lax.dot_general(left, right, (((1,), (1,)), ((), ())), preferred_element_type=jnp.float32)
            result[pl.ds(start, group), :, n * step : (n + 1) * step] = acc.astype(result.dtype).reshape(group, occ, step)
            for h, (at, size) in enumerate(cuts):
                if (n + 1) * step == at + size:
                    for j in range(group):

                        @pl.when(start + j < end)
                        def _():
                            cols = pl.ds(at, size)
                            pltpu.make_async_copy(result.at[start + j, :, cols], out.at[tile(j), :, cols], sem_o.at[h, start + j]).start()

    some = jnp.maximum(lax.shift_right_logical(count + 1, 2), 1)

    @pl.loop(0, some)
    def _(turn):
        last = turn == some - 1
        six = last & (count - turn * 4 > 4)

        @pl.when(jnp.logical_not(six))
        def _():
            one_pass(4, turn * 4, count)

        @pl.when(six)
        def _():
            one_pass(6, turn * 4, count)

    for s in range(16):

        @pl.when(s < count)
        def _():
            for h in range(2):
                cols = pl.ds(*cuts[h])
                pltpu.make_async_copy(result.at[s, :, cols], out.at[order[s], :, cols], sem_o.at[h, s]).wait()

        @pl.when(source[s] == 0)
        def _():
            pltpu.make_async_copy(zero, out.at[s], sem_z.at[s]).wait()


def product(code, local, arrived, pieces):
    occ, width = local.shape[1:]
    return pl.pallas_call(
        product_kernel,
        out_shape=jax.ShapeDtypeStruct((16, occ, width), BF16),
        in_specs=[SMEM] + [ANY] * (2 + len(pieces)),
        out_specs=ANY,
        scratch_shapes=[
            pltpu.VMEM((16, occ, width), BF16),
            pltpu.VMEM((width, width), BF16),
            pltpu.VMEM((18, occ, width), BF16),
            pltpu.VMEM((occ, width), BF16),
            pltpu.SMEM((16,), jnp.int32),
            pltpu.SMEM((16,), jnp.int32),
            pltpu.SemaphoreType.DMA((16,)),
            pltpu.SemaphoreType.DMA((2, 16)),
            pltpu.SemaphoreType.DMA((2, 16)),
            pltpu.SemaphoreType.DMA((16,)),
        ],
        compiler_params=pltpu.CompilerParams(vmem_limit_bytes=56 << 20),
        cost_estimate=pl.CostEstimate(flops=2 * 832 * width * width, bytes_accessed=20_000_000, transcendentals=0),
    )(code, local, arrived, *pieces)


def index(y, z, c):
    return ((y % Y) * Y + z % Y) * 2 + c


def permutation(move):
    return [(index(y, z, c), index(*move(y, z, c))) for y in range(Y) for z in range(Y) for c in range(2)]


SWAP = permutation(lambda y, z, c: (y, z, 1 - c))


def first(s):
    return permutation(lambda y, z, c: (y + s, z, c) if c == 0 else (y, z + s, c))


def second(s):
    return permutation(lambda y, z, c: (y, z + s, c) if c == 0 else (y + s, z, c))


def send(x, pairs):
    return lax.ppermute(x, "blk", pairs)


def ring(x, s):
    return lax.ppermute(x, "grp", [(g, (g + s) % 4) for g in range(4)])


def rows_of_chip(integrals):
    core = lax.axis_index("blk") % 2
    half = integrals.shape[1] // 2
    sibling = send(integrals, SWAP)
    mine = jnp.where(core == 0, integrals[:, :half], integrals[:, half:])
    its = jnp.where(core == 0, sibling[:, :half], sibling[:, half:])
    return jnp.concatenate([jnp.where(core == 0, mine, its), jnp.where(core == 0, its, mine)], 0)


def gather(own):
    before, behind = send(own, first(1)), send(own, first(-1))
    opposite = send(before, first(1))
    near, wide = jnp.stack([own, before]), jnp.stack([behind, opposite])
    near_up, wide_down = send(near, second(1)), send(wide, second(-1))
    wide_up, near_down = send(wide, second(1)), send(near, second(-1))
    near_far, wide_far = send(near_up, second(1)), send(wide_down, second(-1))
    moved = [near_up, wide_down, wide_up, near_down, near_far, wide_far]
    mine = [near, wide] + moved
    return mine + [send(m, SWAP) for m in mine]


def as_one(owners, f, *args):
    empty = lambda *a: jax.tree.map(lambda x: jnp.zeros(x.shape, x.dtype), jax.eval_shape(f, *a))
    return lax.cond(owners[0, 0] >= 0, f, empty, *args)


def body(t2, t2_shape, owners, integrals):
    code, out = pack(owners[:, 0], t2_shape[:, 0], t2)
    arrived = lax.all_to_all(out, "grp", split_axis=0, concat_axis=0, tiled=True)
    pieces = as_one(owners, gather, rows_of_chip(integrals))
    return product(code, t2, arrived, pieces)


def solution(mesh):
    in_specs = (
        P(("grp", "blk"), None, None),
        P(("grp", "blk"), None),
        P(("grp", "blk"), None),
        P("blk", None),
    )
    out_specs = P(("grp", "blk"), None, None)
    return jax.shard_map(body, mesh=mesh, in_specs=in_specs, out_specs=out_specs, check_vma=False)
```

profile of v0, /device:TPU:118, one launch (start us, length us, event | category | flops | bytes accessed | tf_op | source)
XLA Modules:
  0.0 79.5 jit_solution(1679669717899242969)
XLA Ops:
  0.0 3.2 %shard_map.46 = (s32[8]{0:T(128)}, bf16[4,4,64,2304]{3,2,1,0:T(8,128)(2,1)}) custom-call(s32[8]{0:T(128)} %bitcast.13, s32[8]{0:T(128)} %bitcast.12, bf16[8,64,2304]{2,1,0:T(8,128)(2,1)} %local.1), custom_call_target="tpu_custom_call" | custom-call | bytes 4700000 | tf_op jit(solution)/shard_map/pallas_call | solution.py:70
  3.2 0.0 copy-start
  3.2 0.0 copy-start.1
  3.2 5.5 %all-to-all-start = ((bf16[4,4,64,2304]{3,2,1,0:T(8,128)(2,1)}), bf16[4,4,64,2304]{3,2,1,0:T(8,128)(2,1)}, u32[]{:S(2)}, u32[]{:S(2)}) async-start(bf16[4,4,64,2304]{3,2,1,0:T(8,128)(2,1)} %get-tuple-element.25), calls=%async_computation | async-start | bytes 9437184 | tf_op jit(solution)/shard_map/all_to_all | solution.py:291
  8.7 0.0 collective-permute-start.17
  8.8 1.6 %collective-permute-done.17 = bf16[72,2304]{1,0:T(8,128)(2,1)S(1)} collective-permute-done((bf16[72,2304]{1,0:T(8,128)(2,1)S(1)}, bf16[72,2304]{1,0:T(8,128)(2,1)S(1)}, u32[]{:S(2)}, u32[]{:S(2)}) %collective-permute-start.17) | collective-permute-done | bytes 331808 | tf_op jit(solution)/shard_map/ppermute | solution.py:256
  10.4 0.1 broadcast_select_fusion.1
  10.5 44.9 %conditional.1 = (bf16[2,144,1152]{2,1,0:T(8,128)(2,1)}, bf16[2,144,1152]{2,1,0:T(8,128)(2,1)}, bf16[2,144,1152]{2,1,0:T(8,128)(2,1)}, bf16[2,144,1152]{2,1,0:T(...) conditional(s32[]{:T(128)} %bitcast.6, () %tuple.13, ...), branch_computations={%region_0.1_spmd, %region_1.2_spmd} | conditional | flops 663552 | bytes 43795240 | solution.py:286
  10.5 1.3 %collective-permute-start = (bf16[144,1152]{1,0:T(8,128)(2,1)S(1)}, bf16[144,1152]{1,0:T(8,128)(2,1)S(1)}, u32[]{:S(2)}, u32[]{:S(2)}) collective-permute-start(bf16[144,1152]{1,0:T(8,128)(2,1)S(1)} %param.1), channel_id=1, source_target_pairs={{0,8},{1,3},{2,10},{3,5},{4,12},{5,7},{6,14},{7,1},{8,16},{9,11},{... | collective-permute-start | bytes 995336 | tf_op jit(solution)/shard_map/cond/branch_1_fun/ppermute | solution.py:256
  11.8 0.8 collective-permute-start.1
  12.6 5.1 %collective-permute-done = bf16[144,1152]{1,0:T(8,128)(2,1)S(1)} collective-permute-done((bf16[144,1152]{1,0:T(8,128)(2,1)S(1)}, bf16[144,1152]{1,0:T(8,128)(2,1)S(1)}, u32[]{:S(2)}, u32[]{:S(2)}) %collective-permute-start) | collective-permute-done | bytes 331808 | tf_op jit(solution)/shard_map/cond/branch_1_fun/ppermute | solution.py:256
  17.7 1.2 %collective-permute-start.2 = (bf16[144,1152]{1,0:T(8,128)(2,1)S(1)}, bf16[144,1152]{1,0:T(8,128)(2,1)S(1)}, u32[]{:S(2)}, u32[]{:S(2)}) collective-permute-start(bf16[144,1152]{1,0:T(8,128)(2,1)S(1)} %collective-permute-done), channel_id=1, source_target_pairs={{0,8},{1,3},{2,10},{3,5},{4,12},{5,7},{6,14},{7,1},{8,16},{9,11},{... | collective-permute-start | bytes 995336 | tf_op jit(solution)/shard_map/cond/branch_1_fun/ppermute | solution.py:256
  18.9 0.9 %pad_maximum_fusion = bf16[2,144,1152]{2,1,0:T(8,128)(2,1)} fusion(bf16[1,144,1152]{2,1,0:T(8,128)(2,1)S(1)} %bitcast.10, bf16[1,144,1152]{2,1,0:T(8,128)(2,1)S(1)} %bitcast.8), kind=kLoop, calls=%fused_computation | loop fusion | flops 331776 | bytes 1327104 | tf_op jit(solution)/shard_map/cond/branch_1_fun/stack | solution.py:275
  19.8 0.0 collective-permute-start.3
  19.8 2.0 %collective-permute-start.6 = (bf16[2,144,1152]{2,1,0:T(8,128)(2,1)}, bf16[2,144,1152]{2,1,0:T(8,128)(2,1)}, u32[]{:S(2)}, u32[]{:S(2)}) collective-permute-start(bf16[2,144,1152]{2,1,0:T(8,128)(2,1)} %pad_maximum_fusion), channel_id=1, source_target_pairs={{0,6},{1,25},{2,0},{3,27},{4,2},{5,29},{6,4},{7,31},{8,14},{9,1},{... | collective-permute-start | bytes 1990664 | tf_op jit(solution)/shard_map/cond/branch_1_fun/ppermute | solution.py:256
  21.9 0.0 collective-permute-start.9
  21.9 0.0 collective-permute-done.1
  21.9 5.8 %collective-permute-done.2 = bf16[144,1152]{1,0:T(8,128)(2,1)S(1)} collective-permute-done((bf16[144,1152]{1,0:T(8,128)(2,1)S(1)}, bf16[144,1152]{1,0:T(8,128)(2,1)S(1)}, u32[]{:S(2)}, u32[]{:S(2)}) %collective-permute-start.2) | collective-permute-done | bytes 331808 | tf_op jit(solution)/shard_map/cond/branch_1_fun/ppermute | solution.py:256
  27.6 0.9 %pad_maximum_fusion.1 = bf16[2,144,1152]{2,1,0:T(8,128)(2,1)} fusion(bf16[1,144,1152]{2,1,0:T(8,128)(2,1)S(1)} %bitcast.11, bf16[1,144,1152]{2,1,0:T(8,128)(2,1)S(1)} %bitcast.9), kind=kLoop, calls=%fused_computation.1 | loop fusion | flops 331776 | bytes 1327104 | tf_op jit(solution)/shard_map/cond/branch_1_fun/stack | solution.py:275
  28.5 0.0 collective-permute-start.4
  28.5 3.2 %collective-permute-start.5 = (bf16[2,144,1152]{2,1,0:T(8,128)(2,1)}, bf16[2,144,1152]{2,1,0:T(8,128)(2,1)}, u32[]{:S(2)}, u32[]{:S(2)}) collective-permute-start(bf16[2,144,1152]{2,1,0:T(8,128)(2,1)} %pad_maximum_fusion.1), channel_id=1, source_target_pairs={{0,2},{1,9},{2,4},{3,11},{4,6},{5,13},{6,0},{7,15},{8,10},{9,17},{... | collective-permute-start | bytes 1990664 | tf_op jit(solution)/shard_map/cond/branch_1_fun/ppermute | solution.py:256
  31.8 0.4 collective-permute-start.10
  32.1 1.0 %collective-permute-start.7 = (bf16[2,144,1152]{2,1,0:T(8,128)(2,1)}, bf16[2,144,1152]{2,1,0:T(8,128)(2,1)}, u32[]{:S(2)}, u32[]{:S(2)}) collective-permute-start(bf16[2,144,1152]{2,1,0:T(8,128)(2,1)} %collective-permute-done.3), channel_id=1, source_target_pairs={{0,2},{1,9},{2,4},{3,11},{4,6},{5,13},{6,0},{7,15},{8,10},{9,17},{... | collective-permute-start | bytes 1990664 | tf_op jit(solution)/shard_map/cond/branch_1_fun/ppermute | solution.py:256
  33.2 0.1 collective-permute-start.11
  33.2 7.5 %collective-permute-done.4 = bf16[2,144,1152]{2,1,0:T(8,128)(2,1)} collective-permute-done((bf16[2,144,1152]{2,1,0:T(8,128)(2,1)}, bf16[2,144,1152]{2,1,0:T(8,128)(2,1)}, u32[]{:S(2)}, u32[]{:S(2)}) %collective-permute-start.4) | collective-permute-done | bytes 663584 | tf_op jit(solution)/shard_map/cond/branch_1_fun/ppermute | solution.py:256
  40.8 0.5 collective-permute-start.12
  41.3 6.1 %collective-permute-done.7 = bf16[2,144,1152]{2,1,0:T(8,128)(2,1)} collective-permute-done((bf16[2,144,1152]{2,1,0:T(8,128)(2,1)}, bf16[2,144,1152]{2,1,0:T(8,128)(2,1)}, u32[]{:S(2)}, u32[]{:S(2)}) %collective-permute-start.7) | collective-permute-done | bytes 663584 | tf_op jit(solution)/shard_map/cond/branch_1_fun/ppermute | solution.py:256
  47.4 0.5 collective-permute-start.15
  47.9 5.0 %collective-permute-done.8 = bf16[2,144,1152]{2,1,0:T(8,128)(2,1)} collective-permute-done((bf16[2,144,1152]{2,1,0:T(8,128)(2,1)}, bf16[2,144,1152]{2,1,0:T(8,128)(2,1)}, u32[]{:S(2)}, u32[]{:S(2)}) %collective-permute-start.8) | collective-permute-done | bytes 663584 | tf_op jit(solution)/shard_map/cond/branch_1_fun/ppermute | solution.py:256
  53.0 2.4 %collective-permute-done.16 = bf16[2,144,1152]{2,1,0:T(8,128)(2,1)} collective-permute-done((bf16[2,144,1152]{2,1,0:T(8,128)(2,1)}, bf16[2,144,1152]{2,1,0:T(8,128)(2,1)}, u32[]{:S(2)}, u32[]{:S(2)}) %collective-permute-start.16) | collective-permute-done | bytes 663584 | tf_op jit(solution)/shard_map/cond/branch_1_fun/ppermute | solution.py:256
  55.4 6.0 %all-to-all-done.arrived = bf16[4,4,64,2304]{3,2,1,0:T(8,128)(2,1)} async-done(((bf16[4,4,64,2304]{3,2,1,0:T(8,128)(2,1)}), bf16[4,4,64,2304]{3,2,1,0:T(8,128)(2,1)}, u32[]{:S(2)}, u32[]{:S(2)}) %all-to-all-start) | async-done | bytes 4718624 | tf_op jit(solution)/shard_map/all_to_all | solution.py:291
  61.3 18.0 %shard_map.47 = bf16[16,64,2304]{2,1,0:T(8,128)(2,1)} custom-call(s32[8]{0:T(128)} %get-tuple-element.24.code, bf16[8,64,2304]{2,1,0:T(8,128)(2,1)} %local.1, bf16[4,4,64,2304]{3,2,1,0:T(8,128)(2,1)} %all-to-all-done.arrived, bf16[2,144,1152]{2,1,0:T(8,128)(2,1)} %get-tuple-element.26.refs_0_, bf16[2,144,1152]{2,1,0:T(8,128)(2,1)} %get-tuple-element.27.refs_1_, ...), custom_call_target="tpu_custom_call" | custom-call | flops 8833204224 | bytes 20000000 | tf_op jit(solution)/shard_map/pallas_call | solution.py:214
  (17 shorter events, 0.1 us)
Async XLA Ops:
  3.2 5.6 %copy-start = (bf16[72,2304]{1,0:T(8,128)(2,1)S(1)}, bf16[72,2304]{1,0:T(8,128)(2,1)}, u32[]{:S(2)}) copy-start(bf16[72,2304]{1,0:T(8,128)(2,1)} %param.9) | copy-start | bytes 995332
  3.2 5.6 %copy-start.1 = (s32[8,1]{0,1:T(1,128)S(1)}, s32[8,1]{0,1:T(1,128)}, u32[]{:S(2)}) copy-start(s32[8,1]{0,1:T(1,128)} %param.8) | copy-start | bytes 100
  3.2 58.1 %all-to-all-start = ((bf16[4,4,64,2304]{3,2,1,0:T(8,128)(2,1)}), bf16[4,4,64,2304]{3,2,1,0:T(8,128)(2,1)}, u32[]{:S(2)}, u32[]{:S(2)}) async-start(bf16[4,4,64,2304]{3,2,1,0:T(8,128)(2,1)} %get-tuple-element.25), calls=%async_computation | async-start | bytes 9437184 | tf_op jit(solution)/shard_map/all_to_all | solution.py:291
  8.7 1.6 %collective-permute-start.17 = (bf16[72,2304]{1,0:T(8,128)(2,1)S(1)}, bf16[72,2304]{1,0:T(8,128)(2,1)S(1)}, u32[]{:S(2)}, u32[]{:S(2)}) collective-permute-start(bf16[72,2304]{1,0:T(8,128)(2,1)S(1)} %copy-done), channel_id=1, source_target_pairs={{0,1},{1,0},{2,3},{3,2},{4,5},{5,4},{6,7},{7,6},{8,9},{9,8},{10,11... | collective-permute-start | bytes 995336 | tf_op jit(solution)/shard_map/ppermute | solution.py:256
  10.5 7.2 %collective-permute-start = (bf16[144,1152]{1,0:T(8,128)(2,1)S(1)}, bf16[144,1152]{1,0:T(8,128)(2,1)S(1)}, u32[]{:S(2)}, u32[]{:S(2)}) collective-permute-start(bf16[144,1152]{1,0:T(8,128)(2,1)S(1)} %param.1), channel_id=1, source_target_pairs={{0,8},{1,3},{2,10},{3,5},{4,12},{5,7},{6,14},{7,1},{8,16},{9,11},{... | collective-permute-start | bytes 995336 | tf_op jit(solution)/shard_map/cond/branch_1_fun/ppermute | solution.py:256
  11.8 10.1 %collective-permute-start.1 = (bf16[144,1152]{1,0:T(8,128)(2,1)S(1)}, bf16[144,1152]{1,0:T(8,128)(2,1)S(1)}, u32[]{:S(2)}, u32[]{:S(2)}) collective-permute-start(bf16[144,1152]{1,0:T(8,128)(2,1)S(1)} %param.1), channel_id=1, source_target_pairs={{0,24},{1,7},{2,26},{3,1},{4,28},{5,3},{6,30},{7,5},{8,0},{9,15},{... | collective-permute-start | bytes 995336 | tf_op jit(solution)/shard_map/cond/branch_1_fun/ppermute | solution.py:256
  17.7 9.9 %collective-permute-start.2 = (bf16[144,1152]{1,0:T(8,128)(2,1)S(1)}, bf16[144,1152]{1,0:T(8,128)(2,1)S(1)}, u32[]{:S(2)}, u32[]{:S(2)}) collective-permute-start(bf16[144,1152]{1,0:T(8,128)(2,1)S(1)} %collective-permute-done), channel_id=1, source_target_pairs={{0,8},{1,3},{2,10},{3,5},{4,12},{5,7},{6,14},{7,1},{8,16},{9,11},{... | collective-permute-start | bytes 995336 | tf_op jit(solution)/shard_map/cond/branch_1_fun/ppermute | solution.py:256
  19.8 11.9 %collective-permute-start.3 = (bf16[2,144,1152]{2,1,0:T(8,128)(2,1)}, bf16[2,144,1152]{2,1,0:T(8,128)(2,1)}, u32[]{:S(2)}, u32[]{:S(2)}) collective-permute-start(bf16[2,144,1152]{2,1,0:T(8,128)(2,1)} %pad_maximum_fusion), channel_id=1, source_target_pairs={{0,2},{1,9},{2,4},{3,11},{4,6},{5,13},{6,0},{7,15},{8,10},{9,17},{... | collective-permute-start | bytes 1990664 | tf_op jit(solution)/shard_map/cond/branch_1_fun/ppermute | solution.py:256
  19.8 12.3 %collective-permute-start.6 = (bf16[2,144,1152]{2,1,0:T(8,128)(2,1)}, bf16[2,144,1152]{2,1,0:T(8,128)(2,1)}, u32[]{:S(2)}, u32[]{:S(2)}) collective-permute-start(bf16[2,144,1152]{2,1,0:T(8,128)(2,1)} %pad_maximum_fusion), channel_id=1, source_target_pairs={{0,6},{1,25},{2,0},{3,27},{4,2},{5,29},{6,4},{7,31},{8,14},{9,1},{... | collective-permute-start | bytes 1990664 | tf_op jit(solution)/shard_map/cond/branch_1_fun/ppermute | solution.py:256
  21.9 11.3 %collective-permute-start.9 = (bf16[2,144,1152]{2,1,0:T(8,128)(2,1)}, bf16[2,144,1152]{2,1,0:T(8,128)(2,1)}, u32[]{:S(2)}, u32[]{:S(2)}) collective-permute-start(bf16[2,144,1152]{2,1,0:T(8,128)(2,1)} %pad_maximum_fusion), channel_id=1, source_target_pairs={{0,1},{1,0},{2,3},{3,2},{4,5},{5,4},{6,7},{7,6},{8,9},{9,8},{10,11... | collective-permute-start | bytes 1990664 | tf_op jit(solution)/shard_map/cond/branch_1_fun/ppermute | solution.py:256
  28.5 12.2 %collective-permute-start.4 = (bf16[2,144,1152]{2,1,0:T(8,128)(2,1)}, bf16[2,144,1152]{2,1,0:T(8,128)(2,1)}, u32[]{:S(2)}, u32[]{:S(2)}) collective-permute-start(bf16[2,144,1152]{2,1,0:T(8,128)(2,1)} %pad_maximum_fusion.1), channel_id=1, source_target_pairs={{0,6},{1,25},{2,0},{3,27},{4,2},{5,29},{6,4},{7,31},{8,14},{9,1},{... | collective-permute-start | bytes 1990664 | tf_op jit(solution)/shard_map/cond/branch_1_fun/ppermute | solution.py:256
  28.5 12.2 %collective-permute-start.5 = (bf16[2,144,1152]{2,1,0:T(8,128)(2,1)}, bf16[2,144,1152]{2,1,0:T(8,128)(2,1)}, u32[]{:S(2)}, u32[]{:S(2)}) collective-permute-start(bf16[2,144,1152]{2,1,0:T(8,128)(2,1)} %pad_maximum_fusion.1), channel_id=1, source_target_pairs={{0,2},{1,9},{2,4},{3,11},{4,6},{5,13},{6,0},{7,15},{8,10},{9,17},{... | collective-permute-start | bytes 1990664 | tf_op jit(solution)/shard_map/cond/branch_1_fun/ppermute | solution.py:256
  31.8 9.0 %collective-permute-start.10 = (bf16[2,144,1152]{2,1,0:T(8,128)(2,1)}, bf16[2,144,1152]{2,1,0:T(8,128)(2,1)}, u32[]{:S(2)}, u32[]{:S(2)}) collective-permute-start(bf16[2,144,1152]{2,1,0:T(8,128)(2,1)} %pad_maximum_fusion.1), channel_id=1, source_target_pairs={{0,1},{1,0},{2,3},{3,2},{4,5},{5,4},{6,7},{7,6},{8,9},{9,8},{10,11... | collective-permute-start | bytes 1990664 | tf_op jit(solution)/shard_map/cond/branch_1_fun/ppermute | solution.py:256
  32.1 15.3 %collective-permute-start.7 = (bf16[2,144,1152]{2,1,0:T(8,128)(2,1)}, bf16[2,144,1152]{2,1,0:T(8,128)(2,1)}, u32[]{:S(2)}, u32[]{:S(2)}) collective-permute-start(bf16[2,144,1152]{2,1,0:T(8,128)(2,1)} %collective-permute-done.3), channel_id=1, source_target_pairs={{0,2},{1,9},{2,4},{3,11},{4,6},{5,13},{6,0},{7,15},{8,10},{9,17},{... | collective-permute-start | bytes 1990664 | tf_op jit(solution)/shard_map/cond/branch_1_fun/ppermute | solution.py:256
  33.2 14.2 %collective-permute-start.11 = (bf16[2,144,1152]{2,1,0:T(8,128)(2,1)}, bf16[2,144,1152]{2,1,0:T(8,128)(2,1)}, u32[]{:S(2)}, u32[]{:S(2)}) collective-permute-start(bf16[2,144,1152]{2,1,0:T(8,128)(2,1)} %collective-permute-done.3), channel_id=1, source_target_pairs={{0,1},{1,0},{2,3},{3,2},{4,5},{5,4},{6,7},{7,6},{8,9},{9,8},{10,11... | collective-permute-start | bytes 1990664 | tf_op jit(solution)/shard_map/cond/branch_1_fun/ppermute | solution.py:256
  40.7 12.2 %collective-permute-start.8 = (bf16[2,144,1152]{2,1,0:T(8,128)(2,1)}, bf16[2,144,1152]{2,1,0:T(8,128)(2,1)}, u32[]{:S(2)}, u32[]{:S(2)}) collective-permute-start(bf16[2,144,1152]{2,1,0:T(8,128)(2,1)} %collective-permute-done.4), channel_id=1, source_target_pairs={{0,6},{1,25},{2,0},{3,27},{4,2},{5,29},{6,4},{7,31},{8,14},{9,1},{... | collective-permute-start | bytes 1990664 | tf_op jit(solution)/shard_map/cond/branch_1_fun/ppermute | solution.py:256
  40.7 12.2 %collective-permute-start.14 = (bf16[2,144,1152]{2,1,0:T(8,128)(2,1)}, bf16[2,144,1152]{2,1,0:T(8,128)(2,1)}, u32[]{:S(2)}, u32[]{:S(2)}) collective-permute-start(bf16[2,144,1152]{2,1,0:T(8,128)(2,1)} %collective-permute-done.6), channel_id=1, source_target_pairs={{0,1},{1,0},{2,3},{3,2},{4,5},{5,4},{6,7},{7,6},{8,9},{9,8},{10,11... | collective-permute-start | bytes 1990664 | tf_op jit(solution)/shard_map/cond/branch_1_fun/ppermute | solution.py:256
  40.8 12.2 %collective-permute-start.12 = (bf16[2,144,1152]{2,1,0:T(8,128)(2,1)}, bf16[2,144,1152]{2,1,0:T(8,128)(2,1)}, u32[]{:S(2)}, u32[]{:S(2)}) collective-permute-start(bf16[2,144,1152]{2,1,0:T(8,128)(2,1)} %collective-permute-done.4), channel_id=1, source_target_pairs={{0,1},{1,0},{2,3},{3,2},{4,5},{5,4},{6,7},{7,6},{8,9},{9,8},{10,11... | collective-permute-start | bytes 1990664 | tf_op jit(solution)/shard_map/cond/branch_1_fun/ppermute | solution.py:256
  47.4 5.6 %collective-permute-start.13 = (bf16[2,144,1152]{2,1,0:T(8,128)(2,1)}, bf16[2,144,1152]{2,1,0:T(8,128)(2,1)}, u32[]{:S(2)}, u32[]{:S(2)}) collective-permute-start(bf16[2,144,1152]{2,1,0:T(8,128)(2,1)} %collective-permute-done.5), channel_id=1, source_target_pairs={{0,1},{1,0},{2,3},{3,2},{4,5},{5,4},{6,7},{7,6},{8,9},{9,8},{10,11... | collective-permute-start | bytes 1990664 | tf_op jit(solution)/shard_map/cond/branch_1_fun/ppermute | solution.py:256
  47.4 5.6 %collective-permute-start.15 = (bf16[2,144,1152]{2,1,0:T(8,128)(2,1)}, bf16[2,144,1152]{2,1,0:T(8,128)(2,1)}, u32[]{:S(2)}, u32[]{:S(2)}) collective-permute-start(bf16[2,144,1152]{2,1,0:T(8,128)(2,1)} %collective-permute-done.7), channel_id=1, source_target_pairs={{0,1},{1,0},{2,3},{3,2},{4,5},{5,4},{6,7},{7,6},{8,9},{9,8},{10,11... | collective-permute-start | bytes 1990664 | tf_op jit(solution)/shard_map/cond/branch_1_fun/ppermute | solution.py:256
  52.9 2.5 %collective-permute-start.16 = (bf16[2,144,1152]{2,1,0:T(8,128)(2,1)}, bf16[2,144,1152]{2,1,0:T(8,128)(2,1)}, u32[]{:S(2)}, u32[]{:S(2)}) collective-permute-start(bf16[2,144,1152]{2,1,0:T(8,128)(2,1)} %collective-permute-done.8), channel_id=1, source_target_pairs={{0,1},{1,0},{2,3},{3,2},{4,5},{5,4},{6,7},{7,6},{8,9},{9,8},{10,11... | collective-permute-start | bytes 1990664 | tf_op jit(solution)/shard_map/cond/branch_1_fun/ppermute | solution.py:256
where the time goes:
time: 79.4 us; the launch traced here: 79.5 us
  waiting for transfers between devices  39.5 us (50%)
  Pallas kernels  21.2 us (27%)
  starting transfers between devices  16.6 us (21%)
  other arithmetic  1.92 us (2%)
    ppermute x18, waiting for transfers between devices, send(): return lax.ppermute(x, 'blk', pairs)  33.5 us
    pallas_call x1, Pallas kernels, product(): pl.pallas_call(product_kernel, out_shape=jax.ShapeDtypeStruct((16, occ, w...  18 us
    ppermute x18, starting transfers between devices, send(): return lax.ppermute(x, 'blk', pairs)  11.1 us
    all_to_all x1, waiting for transfers between devices, body(): lax.all_to_all(out, 'grp', split_axis=0, concat_axis=0, tiled=True)  5.96 us
    all_to_all x1, starting transfers between devices, body(): lax.all_to_all(out, 'grp', split_axis=0, concat_axis=0, tiled=True)  5.53 us
    pallas_call x1, Pallas kernels, pack(): pl.pallas_call(pack_kernel, out_shape=(jax.ShapeDtypeStruct((8,), jnp.int...  3.17 us
    another operation x2, other arithmetic, gather(): near, wide = (jnp.stack([own, before]), jnp.stack([behind, opposite]))  1.83 us
  transfers between devices with their start and end apart: 19, of which 8 were waited for; matrix products, arithmetic and copies ran while one was open for 2% of the time, Pallas kernels for 0%

commit v1 on v0

--- a/solution.py
+++ b/solution.py
@@ -281,15 +281,10 @@
     return mine + [send(m, SWAP) for m in mine]
 
 
-def as_one(owners, f, *args):
-    empty = lambda *a: jax.tree.map(lambda x: jnp.zeros(x.shape, x.dtype), jax.eval_shape(f, *a))
-    return lax.cond(owners[0, 0] >= 0, f, empty, *args)
-
-
 def body(t2, t2_shape, owners, integrals):
     code, out = pack(owners[:, 0], t2_shape[:, 0], t2)
     arrived = lax.all_to_all(out, "grp", split_axis=0, concat_axis=0, tiled=True)
-    pieces = as_one(owners, gather, rows_of_chip(integrals))
+    pieces = gather(rows_of_chip(integrals))
     return product(code, t2, arrived, pieces)
 
 

time: 79.4 us -> 79 us (level)
  the two profiles are of different devices: /device:TPU:118 before, /device:TPU:60 now
where the time goes in v1:
time: 79 us; the launch traced here: 78.1 us
  waiting for transfers between devices  37.4 us (47%)
  Pallas kernels  19.8 us (25%)
  starting transfers between devices  19.4 us (25%)
  local copies, waits for them, and re-layouts  0.9 us (1%)
    ppermute x18, waiting for transfers between devices, send(): return lax.ppermute(x, 'blk', pairs)  27 us
    pallas_call x1, Pallas kernels, product(): pl.pallas_call(product_kernel, out_shape=jax.ShapeDtypeStruct((16, occ, w...  16.6 us
    ppermute x18, starting transfers between devices, send(): return lax.ppermute(x, 'blk', pairs)  13.9 us
    all_to_all x1, waiting for transfers between devices, body(): lax.all_to_all(out, 'grp', split_axis=0, concat_axis=0, tiled=True)  10.4 us
    all_to_all x1, starting transfers between devices, body(): lax.all_to_all(out, 'grp', split_axis=0, concat_axis=0, tiled=True)  5.46 us
    pallas_call x1, Pallas kernels, pack(): pl.pallas_call(pack_kernel, out_shape=(jax.ShapeDtypeStruct((8,), jnp.int...  3.17 us
  transfers between devices with their start and end apart: 19, of which 11 were waited for; matrix products, arithmetic and copies ran while one was open for 0% of the time, Pallas kernels for 4%

profile of v1, /device:TPU:60, one launch (start us, length us, event | category | flops | bytes accessed | tf_op | source)
XLA Modules:
  0.0 78.1 jit_solution(2500876700823337889)
XLA Ops:
  0.0 3.2 %shard_map.46 = (s32[8]{0:T(128)}, bf16[4,4,64,2304]{3,2,1,0:T(8,128)(2,1)}) custom-call(s32[8]{0:T(128)} %bitcast.10, s32[8]{0:T(128)} %bitcast.11, bf16[8,64,2304]{2,1,0:T(8,128)(2,1)} %local.1), custom_call_target="tpu_custom_call" | custom-call | bytes 4700000 | tf_op jit(solution)/shard_map/pallas_call | solution.py:70
  3.2 0.0 copy-start.2
  3.2 5.5 %all-to-all-start = ((bf16[4,4,64,2304]{3,2,1,0:T(8,128)(2,1)}), bf16[4,4,64,2304]{3,2,1,0:T(8,128)(2,1)}, u32[]{:S(2)}, u32[]{:S(2)}) async-start(bf16[4,4,64,2304]{3,2,1,0:T(8,128)(2,1)} %get-tuple-element.8), calls=%async_computation | async-start | bytes 9437184 | tf_op jit(solution)/shard_map/all_to_all | solution.py:286
  8.7 0.1 broadcast_select_fusion.1
  8.7 0.1 fusion
  8.8 0.4 collective-permute-start.1
  9.1 1.7 %collective-permute-start.2 = (bf16[144,1152]{1,0:T(8,128)(2,1)S(1)}, bf16[144,1152]{1,0:T(8,128)(2,1)S(1)}, u32[]{:S(2)}, u32[]{:S(2)}) collective-permute-start(bf16[144,1152]{1,0:T(8,128)(2,1)S(1)} %get-tuple-element.12), channel_id=1, source_target_pairs={{0,24},{1,7},{2,26},{3,1},{4,28},{5,3},{6,30},{7,5},{8,0},{9,15},{... | collective-permute-start | bytes 995336 | tf_op jit(solution)/shard_map/ppermute | solution.py:256
  10.9 5.1 %collective-permute-done.1 = bf16[144,1152]{1,0:T(8,128)(2,1)S(1)} collective-permute-done((bf16[144,1152]{1,0:T(8,128)(2,1)S(1)}, bf16[144,1152]{1,0:T(8,128)(2,1)S(1)}, u32[]{:S(2)}, u32[]{:S(2)}) %collective-permute-start.1) | collective-permute-done | bytes 331808 | tf_op jit(solution)/shard_map/ppermute | solution.py:256
  16.0 1.5 %collective-permute-start.3 = (bf16[144,1152]{1,0:T(8,128)(2,1)S(1)}, bf16[144,1152]{1,0:T(8,128)(2,1)S(1)}, u32[]{:S(2)}, u32[]{:S(2)}) collective-permute-start(bf16[144,1152]{1,0:T(8,128)(2,1)S(1)} %collective-permute-done.1), channel_id=1, source_target_pairs={{0,8},{1,3},{2,10},{3,5},{4,12},{5,7},{6,14},{7,1},{8,16},{9,11},{... | collective-permute-start | bytes 995336 | tf_op jit(solution)/shard_map/ppermute | solution.py:256
  17.5 0.1 pad_maximum_fusion.refs_0_
  17.6 2.0 %collective-permute-start.4 = (bf16[2,144,1152]{2,1,0:T(8,128)(2,1)S(1)}, bf16[2,144,1152]{2,1,0:T(8,128)(2,1)S(1)}, u32[]{:S(2)}, u32[]{:S(2)}) collective-permute-start(bf16[2,144,1152]{2,1,0:T(8,128)(2,1)S(1)} %pad_maximum_fusion.refs_0_), channel_id=1, source_target_pairs={{0,2},{1,9},{2,4},{3,11},{4,6},{5,13},{6,0},{7,15},{8,10},{9,17},{... | collective-permute-start | bytes 1990664 | tf_op jit(solution)/shard_map/ppermute | solution.py:256
  19.5 0.1 collective-permute-start.7
  19.7 6.7 %collective-permute-done.3 = bf16[144,1152]{1,0:T(8,128)(2,1)S(1)} collective-permute-done((bf16[144,1152]{1,0:T(8,128)(2,1)S(1)}, bf16[144,1152]{1,0:T(8,128)(2,1)S(1)}, u32[]{:S(2)}, u32[]{:S(2)}) %collective-permute-start.3) | collective-permute-done | bytes 331808 | tf_op jit(solution)/shard_map/ppermute | solution.py:256
  26.3 0.1 pad_maximum_fusion.1.refs_1_
  26.4 0.1 collective-permute-start.5
  26.5 2.2 %collective-permute-start.6 = (bf16[2,144,1152]{2,1,0:T(8,128)(2,1)S(1)}, bf16[2,144,1152]{2,1,0:T(8,128)(2,1)S(1)}, u32[]{:S(2)}, u32[]{:S(2)}) collective-permute-start(bf16[2,144,1152]{2,1,0:T(8,128)(2,1)S(1)} %pad_maximum_fusion.1.refs_1_), channel_id=1, source_target_pairs={{0,2},{1,9},{2,4},{3,11},{4,6},{5,13},{6,0},{7,15},{8,10},{9,17},{... | collective-permute-start | bytes 1990664 | tf_op jit(solution)/shard_map/ppermute | solution.py:256
  28.7 0.5 collective-permute-done.4.refs_2_
  29.2 1.2 %collective-permute-start.11 = (bf16[2,144,1152]{2,1,0:T(8,128)(2,1)S(1)}, bf16[2,144,1152]{2,1,0:T(8,128)(2,1)S(1)}, u32[]{:S(2)}, u32[]{:S(2)}) collective-permute-start(bf16[2,144,1152]{2,1,0:T(8,128)(2,1)S(1)} %pad_maximum_fusion.1.refs_1_), channel_id=1, source_target_pairs={{0,1},{1,0},{2,3},{3,2},{4,5},{5,4},{6,7},{7,6},{8,9},{9,8},{10,11... | collective-permute-start | bytes 1990664 | tf_op jit(solution)/shard_map/ppermute | solution.py:256
  30.4 1.9 %collective-permute-start.8 = (bf16[2,144,1152]{2,1,0:T(8,128)(2,1)S(1)}, bf16[2,144,1152]{2,1,0:T(8,128)(2,1)S(1)}, u32[]{:S(2)}, u32[]{:S(2)}) collective-permute-start(bf16[2,144,1152]{2,1,0:T(8,128)(2,1)S(1)} %collective-permute-done.4.refs_2_), channel_id=1, source_target_pairs={{0,2},{1,9},{2,4},{3,11},{4,6},{5,13},{6,0},{7,15},{8,10},{9,17},{... | collective-permute-start | bytes 1990664 | tf_op jit(solution)/shard_map/ppermute | solution.py:256
  32.3 5.0 %collective-permute-done.5.refs_3_ = bf16[2,144,1152]{2,1,0:T(8,128)(2,1)S(1)} collective-permute-done((bf16[2,144,1152]{2,1,0:T(8,128)(2,1)S(1)}, bf16[2,144,1152]{2,1,0:T(8,128)(2,1)S(1)}, u32[]{:S(2)}, u32[]{:S(2)}) %collective-permute-start.5) | collective-permute-done | bytes 663584 | tf_op jit(solution)/shard_map/ppermute | solution.py:256
  37.3 1.8 %collective-permute-start.9 = (bf16[2,144,1152]{2,1,0:T(8,128)(2,1)S(1)}, bf16[2,144,1152]{2,1,0:T(8,128)(2,1)S(1)}, u32[]{:S(2)}, u32[]{:S(2)}) collective-permute-start(bf16[2,144,1152]{2,1,0:T(8,128)(2,1)S(1)} %collective-permute-done.5.refs_3_), channel_id=1, source_target_pairs={{0,6},{1,25},{2,0},{3,27},{4,2},{5,29},{6,4},{7,31},{8,14},{9,1},{... | collective-permute-start | bytes 1990664 | tf_op jit(solution)/shard_map/ppermute | solution.py:256
  39.2 0.5 collective-permute-done.6.refs_4_
  39.6 0.5 collective-permute-start.13
  40.1 6.6 %collective-permute-done.8.refs_6_ = bf16[2,144,1152]{2,1,0:T(8,128)(2,1)S(1)} collective-permute-done((bf16[2,144,1152]{2,1,0:T(8,128)(2,1)S(1)}, bf16[2,144,1152]{2,1,0:T(8,128)(2,1)S(1)}, u32[]{:S(2)}, u32[]{:S(2)}) %collective-permute-start.8) | collective-permute-done | bytes 663584 | tf_op jit(solution)/shard_map/ppermute | solution.py:256
  46.8 0.5 collective-permute-start.16
  47.3 0.7 collective-permute-done.9.refs_7_
  48.1 0.8 %collective-permute-done.14.refs_12_ = bf16[2,144,1152]{2,1,0:T(8,128)(2,1)S(1)} collective-permute-done((bf16[2,144,1152]{2,1,0:T(8,128)(2,1)S(1)}, bf16[2,144,1152]{2,1,0:T(8,128)(2,1)S(1)}, u32[]{:S(2)}, u32[]{:S(2)}) %collective-permute-start.14) | collective-permute-done | bytes 663584 | tf_op jit(solution)/shard_map/ppermute | solution.py:256
  48.9 0.9 %collective-permute-done.16.refs_14_ = bf16[2,144,1152]{2,1,0:T(8,128)(2,1)S(1)} collective-permute-done((bf16[2,144,1152]{2,1,0:T(8,128)(2,1)S(1)}, bf16[2,144,1152]{2,1,0:T(8,128)(2,1)S(1)}, u32[]{:S(2)}, u32[]{:S(2)}) %collective-permute-start.16) | collective-permute-done | bytes 663584 | tf_op jit(solution)/shard_map/ppermute | solution.py:256
  49.9 0.8 %copy-done.15 = bf16[2,144,1152]{2,1,0:T(8,128)(2,1)} copy-done((bf16[2,144,1152]{2,1,0:T(8,128)(2,1)}, bf16[2,144,1152]{2,1,0:T(8,128)(2,1)S(1)}, u32[]{:S(2)}) %copy-start.15) | copy-done | bytes 663576
  50.7 0.2 collective-permute-done.17.refs_15_
  50.9 10.4 %all-to-all-done.arrived = bf16[4,4,64,2304]{3,2,1,0:T(8,128)(2,1)} async-done(((bf16[4,4,64,2304]{3,2,1,0:T(8,128)(2,1)}), bf16[4,4,64,2304]{3,2,1,0:T(8,128)(2,1)}, u32[]{:S(2)}, u32[]{:S(2)}) %all-to-all-start) | async-done | bytes 4718624 | tf_op jit(solution)/shard_map/all_to_all | solution.py:286
  61.3 16.6 %shard_map.47 = bf16[16,64,2304]{2,1,0:T(8,128)(2,1)} custom-call(s32[8]{0:T(128)} %get-tuple-element.7.code, bf16[8,64,2304]{2,1,0:T(8,128)(2,1)} %local.1, bf16[4,4,64,2304]{3,2,1,0:T(8,128)(2,1)} %all-to-all-done.arrived, bf16[2,144,1152]{2,1,0:T(8,128)(2,1)} %copy-done, bf16[2,144,1152]{2,1,0:T(8,128)(2,1)} %copy-done.1, ...), custom_call_target="tpu_custom_call" | custom-call | flops 8833204224 | bytes 20000000 | tf_op jit(solution)/shard_map/pallas_call | solution.py:214
  (44 shorter events, 0.1 us)
Async XLA Ops:
  0.0 8.7 %collective-permute-start = (bf16[72,2304]{1,0:T(8,128)(2,1)}, bf16[72,2304]{1,0:T(8,128)(2,1)S(1)}, u32[]{:S(2)}, u32[]{:S(2)}) collective-permute-start(bf16[72,2304]{1,0:T(8,128)(2,1)} %param.7), channel_id=1, source_target_pairs={{0,1},{1,0},{2,3},{3,2},{4,5},{5,4},{6,7},{7,6},{8,9},{9,8},{10,11... | collective-permute-start | bytes 995336 | tf_op jit(solution)/shard_map/ppermute | solution.py:256
  3.2 5.5 %copy-start.2 = (bf16[72,2304]{1,0:T(8,128)(2,1)S(1)}, bf16[72,2304]{1,0:T(8,128)(2,1)}, u32[]{:S(2)}) copy-start(bf16[72,2304]{1,0:T(8,128)(2,1)} %param.7) | copy-start | bytes 995332
  3.2 58.1 %all-to-all-start = ((bf16[4,4,64,2304]{3,2,1,0:T(8,128)(2,1)}), bf16[4,4,64,2304]{3,2,1,0:T(8,128)(2,1)}, u32[]{:S(2)}, u32[]{:S(2)}) async-start(bf16[4,4,64,2304]{3,2,1,0:T(8,128)(2,1)} %get-tuple-element.8), calls=%async_computation | async-start | bytes 9437184 | tf_op jit(solution)/shard_map/all_to_all | solution.py:286
  8.8 7.2 %collective-permute-start.1 = (bf16[144,1152]{1,0:T(8,128)(2,1)S(1)}, bf16[144,1152]{1,0:T(8,128)(2,1)S(1)}, u32[]{:S(2)}, u32[]{:S(2)}) collective-permute-start(bf16[144,1152]{1,0:T(8,128)(2,1)S(1)} %get-tuple-element.12), channel_id=1, source_target_pairs={{0,8},{1,3},{2,10},{3,5},{4,12},{5,7},{6,14},{7,1},{8,16},{9,11},{... | collective-permute-start | bytes 995336 | tf_op jit(solution)/shard_map/ppermute | solution.py:256
  9.1 10.5 %collective-permute-start.2 = (bf16[144,1152]{1,0:T(8,128)(2,1)S(1)}, bf16[144,1152]{1,0:T(8,128)(2,1)S(1)}, u32[]{:S(2)}, u32[]{:S(2)}) collective-permute-start(bf16[144,1152]{1,0:T(8,128)(2,1)S(1)} %get-tuple-element.12), channel_id=1, source_target_pairs={{0,24},{1,7},{2,26},{3,1},{4,28},{5,3},{6,30},{7,5},{8,0},{9,15},{... | collective-permute-start | bytes 995336 | tf_op jit(solution)/shard_map/ppermute | solution.py:256
  16.0 10.4 %collective-permute-start.3 = (bf16[144,1152]{1,0:T(8,128)(2,1)S(1)}, bf16[144,1152]{1,0:T(8,128)(2,1)S(1)}, u32[]{:S(2)}, u32[]{:S(2)}) collective-permute-start(bf16[144,1152]{1,0:T(8,128)(2,1)S(1)} %collective-permute-done.1), channel_id=1, source_target_pairs={{0,8},{1,3},{2,10},{3,5},{4,12},{5,7},{6,14},{7,1},{8,16},{9,11},{... | collective-permute-start | bytes 995336 | tf_op jit(solution)/shard_map/ppermute | solution.py:256
  17.5 43.7 %copy-start = (bf16[2,144,1152]{2,1,0:T(8,128)(2,1)}, bf16[2,144,1152]{2,1,0:T(8,128)(2,1)S(1)}, u32[]{:S(2)}) copy-start(bf16[2,144,1152]{2,1,0:T(8,128)(2,1)S(1)} %pad_maximum_fusion.refs_0_) | copy-start | bytes 1990660
  17.6 11.6 %collective-permute-start.4 = (bf16[2,144,1152]{2,1,0:T(8,128)(2,1)S(1)}, bf16[2,144,1152]{2,1,0:T(8,128)(2,1)S(1)}, u32[]{:S(2)}, u32[]{:S(2)}) collective-permute-start(bf16[2,144,1152]{2,1,0:T(8,128)(2,1)S(1)} %pad_maximum_fusion.refs_0_), channel_id=1, source_target_pairs={{0,2},{1,9},{2,4},{3,11},{4,6},{5,13},{6,0},{7,15},{8,10},{9,17},{... | collective-permute-start | bytes 1990664 | tf_op jit(solution)/shard_map/ppermute | solution.py:256
  19.5 10.9 %collective-permute-start.7 = (bf16[2,144,1152]{2,1,0:T(8,128)(2,1)S(1)}, bf16[2,144,1152]{2,1,0:T(8,128)(2,1)S(1)}, u32[]{:S(2)}, u32[]{:S(2)}) collective-permute-start(bf16[2,144,1152]{2,1,0:T(8,128)(2,1)S(1)} %pad_maximum_fusion.refs_0_), channel_id=1, source_target_pairs={{0,6},{1,25},{2,0},{3,27},{4,2},{5,29},{6,4},{7,31},{8,14},{9,1},{... | collective-permute-start | bytes 1990664 | tf_op jit(solution)/shard_map/ppermute | solution.py:256
  19.6 12.7 %collective-permute-start.10 = (bf16[2,144,1152]{2,1,0:T(8,128)(2,1)S(1)}, bf16[2,144,1152]{2,1,0:T(8,128)(2,1)S(1)}, u32[]{:S(2)}, u32[]{:S(2)}) collective-permute-start(bf16[2,144,1152]{2,1,0:T(8,128)(2,1)S(1)} %pad_maximum_fusion.refs_0_), channel_id=1, source_target_pairs={{0,1},{1,0},{2,3},{3,2},{4,5},{5,4},{6,7},{7,6},{8,9},{9,8},{10,11... | collective-permute-start | bytes 1990664 | tf_op jit(solution)/shard_map/ppermute | solution.py:256
  26.4 34.9 %copy-start.1 = (bf16[2,144,1152]{2,1,0:T(8,128)(2,1)}, bf16[2,144,1152]{2,1,0:T(8,128)(2,1)S(1)}, u32[]{:S(2)}) copy-start(bf16[2,144,1152]{2,1,0:T(8,128)(2,1)S(1)} %pad_maximum_fusion.1.refs_1_) | copy-start | bytes 1990660
  26.4 10.9 %collective-permute-start.5 = (bf16[2,144,1152]{2,1,0:T(8,128)(2,1)S(1)}, bf16[2,144,1152]{2,1,0:T(8,128)(2,1)S(1)}, u32[]{:S(2)}, u32[]{:S(2)}) collective-permute-start(bf16[2,144,1152]{2,1,0:T(8,128)(2,1)S(1)} %pad_maximum_fusion.1.refs_1_), channel_id=1, source_target_pairs={{0,6},{1,25},{2,0},{3,27},{4,2},{5,29},{6,4},{7,31},{8,14},{9,1},{... | collective-permute-start | bytes 1990664 | tf_op jit(solution)/shard_map/ppermute | solution.py:256
  26.5 13.1 %collective-permute-start.6 = (bf16[2,144,1152]{2,1,0:T(8,128)(2,1)S(1)}, bf16[2,144,1152]{2,1,0:T(8,128)(2,1)S(1)}, u32[]{:S(2)}, u32[]{:S(2)}) collective-permute-start(bf16[2,144,1152]{2,1,0:T(8,128)(2,1)S(1)} %pad_maximum_fusion.1.refs_1_), channel_id=1, source_target_pairs={{0,2},{1,9},{2,4},{3,11},{4,6},{5,13},{6,0},{7,15},{8,10},{9,17},{... | collective-permute-start | bytes 1990664 | tf_op jit(solution)/shard_map/ppermute | solution.py:256
  29.2 32.1 %copy-start.3 = (bf16[2,144,1152]{2,1,0:T(8,128)(2,1)}, bf16[2,144,1152]{2,1,0:T(8,128)(2,1)S(1)}, u32[]{:S(2)}) copy-start(bf16[2,144,1152]{2,1,0:T(8,128)(2,1)S(1)} %collective-permute-done.4.refs_2_) | copy-start | bytes 1990660
  29.2 10.4 %collective-permute-start.11 = (bf16[2,144,1152]{2,1,0:T(8,128)(2,1)S(1)}, bf16[2,144,1152]{2,1,0:T(8,128)(2,1)S(1)}, u32[]{:S(2)}, u32[]{:S(2)}) collective-permute-start(bf16[2,144,1152]{2,1,0:T(8,128)(2,1)S(1)} %pad_maximum_fusion.1.refs_1_), channel_id=1, source_target_pairs={{0,1},{1,0},{2,3},{3,2},{4,5},{5,4},{6,7},{7,6},{8,9},{9,8},{10,11... | collective-permute-start | bytes 1990664 | tf_op jit(solution)/shard_map/ppermute | solution.py:256
  30.4 30.8 %copy-start.4 = (bf16[2,144,1152]{2,1,0:T(8,128)(2,1)}, bf16[2,144,1152]{2,1,0:T(8,128)(2,1)S(1)}, u32[]{:S(2)}) copy-start(bf16[2,144,1152]{2,1,0:T(8,128)(2,1)S(1)} %collective-permute-done.7.refs_5_) | copy-start | bytes 1990660
  30.4 16.3 %collective-permute-start.8 = (bf16[2,144,1152]{2,1,0:T(8,128)(2,1)S(1)}, bf16[2,144,1152]{2,1,0:T(8,128)(2,1)S(1)}, u32[]{:S(2)}, u32[]{:S(2)}) collective-permute-start(bf16[2,144,1152]{2,1,0:T(8,128)(2,1)S(1)} %collective-permute-done.4.refs_2_), channel_id=1, source_target_pairs={{0,2},{1,9},{2,4},{3,11},{4,6},{5,13},{6,0},{7,15},{8,10},{9,17},{... | collective-permute-start | bytes 1990664 | tf_op jit(solution)/shard_map/ppermute | solution.py:256
  32.3 28.9 %copy-start.5 = (bf16[2,144,1152]{2,1,0:T(8,128)(2,1)}, bf16[2,144,1152]{2,1,0:T(8,128)(2,1)S(1)}, u32[]{:S(2)}) copy-start(bf16[2,144,1152]{2,1,0:T(8,128)(2,1)S(1)} %collective-permute-done.10.refs_8_) | copy-start | bytes 1990660
  32.3 14.4 %collective-permute-start.12 = (bf16[2,144,1152]{2,1,0:T(8,128)(2,1)S(1)}, bf16[2,144,1152]{2,1,0:T(8,128)(2,1)S(1)}, u32[]{:S(2)}, u32[]{:S(2)}) collective-permute-start(bf16[2,144,1152]{2,1,0:T(8,128)(2,1)S(1)} %collective-permute-done.4.refs_2_), channel_id=1, source_target_pairs={{0,1},{1,0},{2,3},{3,2},{4,5},{5,4},{6,7},{7,6},{8,9},{9,8},{10,11... | collective-permute-start | bytes 1990664 | tf_op jit(solution)/shard_map/ppermute | solution.py:256
  37.3 10.7 %copy-start.6 = (bf16[2,144,1152]{2,1,0:T(8,128)(2,1)}, bf16[2,144,1152]{2,1,0:T(8,128)(2,1)S(1)}, u32[]{:S(2)}) copy-start(bf16[2,144,1152]{2,1,0:T(8,128)(2,1)S(1)} %collective-permute-done.5.refs_3_) | copy-start | bytes 1990660
  37.3 10.7 %collective-permute-start.9 = (bf16[2,144,1152]{2,1,0:T(8,128)(2,1)S(1)}, bf16[2,144,1152]{2,1,0:T(8,128)(2,1)S(1)}, u32[]{:S(2)}, u32[]{:S(2)}) collective-permute-start(bf16[2,144,1152]{2,1,0:T(8,128)(2,1)S(1)} %collective-permute-done.5.refs_3_), channel_id=1, source_target_pairs={{0,6},{1,25},{2,0},{3,27},{4,2},{5,29},{6,4},{7,31},{8,14},{9,1},{... | collective-permute-start | bytes 1990664 | tf_op jit(solution)/shard_map/ppermute | solution.py:256
  39.6 8.4 %copy-start.7 = (bf16[2,144,1152]{2,1,0:T(8,128)(2,1)}, bf16[2,144,1152]{2,1,0:T(8,128)(2,1)S(1)}, u32[]{:S(2)}) copy-start(bf16[2,144,1152]{2,1,0:T(8,128)(2,1)S(1)} %collective-permute-done.6.refs_4_) | copy-start | bytes 1990660
  39.6 8.4 %collective-permute-start.15 = (bf16[2,144,1152]{2,1,0:T(8,128)(2,1)S(1)}, bf16[2,144,1152]{2,1,0:T(8,128)(2,1)S(1)}, u32[]{:S(2)}, u32[]{:S(2)}) collective-permute-start(bf16[2,144,1152]{2,1,0:T(8,128)(2,1)S(1)} %collective-permute-done.7.refs_5_), channel_id=1, source_target_pairs={{0,1},{1,0},{2,3},{3,2},{4,5},{5,4},{6,7},{7,6},{8,9},{9,8},{10,11... | collective-permute-start | bytes 1990664 | tf_op jit(solution)/shard_map/ppermute | solution.py:256
  39.6 9.2 %copy-start.8 = (bf16[2,144,1152]{2,1,0:T(8,128)(2,1)}, bf16[2,144,1152]{2,1,0:T(8,128)(2,1)S(1)}, u32[]{:S(2)}) copy-start(bf16[2,144,1152]{2,1,0:T(8,128)(2,1)S(1)} %collective-permute-done.11.refs_9_) | copy-start | bytes 1990660
  39.6 8.4 %collective-permute-start.13 = (bf16[2,144,1152]{2,1,0:T(8,128)(2,1)S(1)}, bf16[2,144,1152]{2,1,0:T(8,128)(2,1)S(1)}, u32[]{:S(2)}, u32[]{:S(2)}) collective-permute-start(bf16[2,144,1152]{2,1,0:T(8,128)(2,1)S(1)} %collective-permute-done.5.refs_3_), channel_id=1, source_target_pairs={{0,1},{1,0},{2,3},{3,2},{4,5},{5,4},{6,7},{7,6},{8,9},{9,8},{10,11... | collective-permute-start | bytes 1990664 | tf_op jit(solution)/shard_map/ppermute | solution.py:256
  46.7 3.1 %copy-start.9 = (bf16[2,144,1152]{2,1,0:T(8,128)(2,1)}, bf16[2,144,1152]{2,1,0:T(8,128)(2,1)S(1)}, u32[]{:S(2)}) copy-start(bf16[2,144,1152]{2,1,0:T(8,128)(2,1)S(1)} %collective-permute-done.8.refs_6_) | copy-start | bytes 1990660
  46.7 2.1 %collective-permute-start.14 = (bf16[2,144,1152]{2,1,0:T(8,128)(2,1)S(1)}, bf16[2,144,1152]{2,1,0:T(8,128)(2,1)S(1)}, u32[]{:S(2)}, u32[]{:S(2)}) collective-permute-start(bf16[2,144,1152]{2,1,0:T(8,128)(2,1)S(1)} %collective-permute-done.6.refs_4_), channel_id=1, source_target_pairs={{0,1},{1,0},{2,3},{3,2},{4,5},{5,4},{6,7},{7,6},{8,9},{9,8},{10,11... | collective-permute-start | bytes 1990664 | tf_op jit(solution)/shard_map/ppermute | solution.py:256
  46.7 3.1 %copy-start.10 = (bf16[2,144,1152]{2,1,0:T(8,128)(2,1)}, bf16[2,144,1152]{2,1,0:T(8,128)(2,1)S(1)}, u32[]{:S(2)}) copy-start(bf16[2,144,1152]{2,1,0:T(8,128)(2,1)S(1)} %collective-permute-done.12.refs_10_) | copy-start | bytes 1990660
  46.8 3.0 %collective-permute-start.16 = (bf16[2,144,1152]{2,1,0:T(8,128)(2,1)S(1)}, bf16[2,144,1152]{2,1,0:T(8,128)(2,1)S(1)}, u32[]{:S(2)}, u32[]{:S(2)}) collective-permute-start(bf16[2,144,1152]{2,1,0:T(8,128)(2,1)S(1)} %collective-permute-done.8.refs_6_), channel_id=1, source_target_pairs={{0,1},{1,0},{2,3},{3,2},{4,5},{5,4},{6,7},{7,6},{8,9},{9,8},{10,11... | collective-permute-start | bytes 1990664 | tf_op jit(solution)/shard_map/ppermute | solution.py:256
  48.0 1.8 %copy-start.11 = (bf16[2,144,1152]{2,1,0:T(8,128)(2,1)}, bf16[2,144,1152]{2,1,0:T(8,128)(2,1)S(1)}, u32[]{:S(2)}) copy-start(bf16[2,144,1152]{2,1,0:T(8,128)(2,1)S(1)} %collective-permute-done.9.refs_7_) | copy-start | bytes 1990660
  48.0 2.9 %collective-permute-start.17 = (bf16[2,144,1152]{2,1,0:T(8,128)(2,1)S(1)}, bf16[2,144,1152]{2,1,0:T(8,128)(2,1)}, u32[]{:S(2)}, u32[]{:S(2)}) collective-permute-start(bf16[2,144,1152]{2,1,0:T(8,128)(2,1)S(1)} %collective-permute-done.9.refs_7_), channel_id=1, source_target_pairs={{0,1},{1,0},{2,3},{3,2},{4,5},{5,4},{6,7},{7,6},{8,9},{9,8},{10,11... | collective-permute-start | bytes 1990664 | tf_op jit(solution)/shard_map/ppermute | solution.py:256
  48.0 1.8 %copy-start.12 = (bf16[2,144,1152]{2,1,0:T(8,128)(2,1)}, bf16[2,144,1152]{2,1,0:T(8,128)(2,1)S(1)}, u32[]{:S(2)}) copy-start(bf16[2,144,1152]{2,1,0:T(8,128)(2,1)S(1)} %collective-permute-done.15.refs_13_) | copy-start | bytes 1990660
  (3 other events, 3.6 us)

commit v2 on v0

--- a/solution.py
+++ b/solution.py
@@ -152,15 +152,16 @@
         def _():
             order[count] = s
 
-        @pl.when(jnp.logical_not(taken))
-        def _():
-            pltpu.make_async_copy(zero, out.at[s], sem_z.at[s]).start()
-
         source[s] = taken.astype(jnp.int32)
         count = count + taken.astype(jnp.int32)
 
     for copy in copies:
         copy.wait()
+    for s in range(16):
+
+        @pl.when(source[s] == 0)
+        def _():
+            pltpu.make_async_copy(zero, out.at[s], sem_z.at[s]).start()
 
     split = (width // step // 2 + 1) * step
     cuts = ((0, split), (split, width - split))

time: 79.4 us -> 78.7 us (level)
  the two profiles are of different devices: /device:TPU:118 before, /device:TPU:68 now
where the time goes in v2:
time: 78.7 us; the launch traced here: 77.4 us
  waiting for transfers between devices  38.2 us (49%)
  Pallas kernels  19.8 us (25%)
  starting transfers between devices  17.1 us (22%)
  other arithmetic  1.92 us (2%)
    ppermute x18, waiting for transfers between devices, send(): return lax.ppermute(x, 'blk', pairs)  34.4 us
    pallas_call x1, Pallas kernels, product(): pl.pallas_call(product_kernel, out_shape=jax.ShapeDtypeStruct((16, occ, w...  16.6 us
    ppermute x18, starting transfers between devices, send(): return lax.ppermute(x, 'blk', pairs)  11.6 us
    all_to_all x1, starting transfers between devices, body(): lax.all_to_all(out, 'grp', split_axis=0, concat_axis=0, tiled=True)  5.59 us
    all_to_all x1, waiting for transfers between devices, body(): lax.all_to_all(out, 'grp', split_axis=0, concat_axis=0, tiled=True)  3.82 us
    pallas_call x1, Pallas kernels, pack(): pl.pallas_call(pack_kernel, out_shape=(jax.ShapeDtypeStruct((8,), jnp.int...  3.12 us
    another operation x2, other arithmetic, gather(): near, wide = (jnp.stack([own, before]), jnp.stack([behind, opposite]))  1.83 us
  transfers between devices with their start and end apart: 19, of which 8 were waited for; matrix products, arithmetic and copies ran while one was open for 2% of the time, Pallas kernels for 0%

profile of v2, /device:TPU:68, one launch (start us, length us, event | category | flops | bytes accessed | tf_op | source)
XLA Modules:
  0.0 77.4 jit_solution(7733828222903012150)
XLA Ops:
  0.0 3.1 %shard_map.46 = (s32[8]{0:T(128)}, bf16[4,4,64,2304]{3,2,1,0:T(8,128)(2,1)}) custom-call(s32[8]{0:T(128)} %bitcast.13, s32[8]{0:T(128)} %bitcast.12, bf16[8,64,2304]{2,1,0:T(8,128)(2,1)} %local.1), custom_call_target="tpu_custom_call" | custom-call | bytes 4700000 | tf_op jit(solution)/shard_map/pallas_call | solution.py:70
  3.1 0.0 copy-start
  3.1 0.0 copy-start.1
  3.2 5.6 %all-to-all-start = ((bf16[4,4,64,2304]{3,2,1,0:T(8,128)(2,1)}), bf16[4,4,64,2304]{3,2,1,0:T(8,128)(2,1)}, u32[]{:S(2)}, u32[]{:S(2)}) async-start(bf16[4,4,64,2304]{3,2,1,0:T(8,128)(2,1)} %get-tuple-element.25), calls=%async_computation | async-start | bytes 9437184 | tf_op jit(solution)/shard_map/all_to_all | solution.py:292
  8.8 1.6 %collective-permute-done.17 = bf16[72,2304]{1,0:T(8,128)(2,1)S(1)} collective-permute-done((bf16[72,2304]{1,0:T(8,128)(2,1)S(1)}, bf16[72,2304]{1,0:T(8,128)(2,1)S(1)}, u32[]{:S(2)}, u32[]{:S(2)}) %collective-permute-start.17) | collective-permute-done | bytes 331808 | tf_op jit(solution)/shard_map/ppermute | solution.py:257
  10.4 0.1 broadcast_select_fusion.1
  10.5 46.3 %conditional.1 = (bf16[2,144,1152]{2,1,0:T(8,128)(2,1)}, bf16[2,144,1152]{2,1,0:T(8,128)(2,1)}, bf16[2,144,1152]{2,1,0:T(8,128)(2,1)}, bf16[2,144,1152]{2,1,0:T(...) conditional(s32[]{:T(128)} %bitcast.6, () %tuple.13, ...), branch_computations={%region_0.1_spmd, %region_1.2_spmd} | conditional | flops 663552 | bytes 43795240 | solution.py:287
  10.5 1.7 %collective-permute-start = (bf16[144,1152]{1,0:T(8,128)(2,1)S(1)}, bf16[144,1152]{1,0:T(8,128)(2,1)S(1)}, u32[]{:S(2)}, u32[]{:S(2)}) collective-permute-start(bf16[144,1152]{1,0:T(8,128)(2,1)S(1)} %param.1), channel_id=1, source_target_pairs={{0,8},{1,3},{2,10},{3,5},{4,12},{5,7},{6,14},{7,1},{8,16},{9,11},{... | collective-permute-start | bytes 995336 | tf_op jit(solution)/shard_map/cond/branch_1_fun/ppermute | solution.py:257
  12.2 1.6 %collective-permute-start.1 = (bf16[144,1152]{1,0:T(8,128)(2,1)S(1)}, bf16[144,1152]{1,0:T(8,128)(2,1)S(1)}, u32[]{:S(2)}, u32[]{:S(2)}) collective-permute-start(bf16[144,1152]{1,0:T(8,128)(2,1)S(1)} %param.1), channel_id=1, source_target_pairs={{0,24},{1,7},{2,26},{3,1},{4,28},{5,3},{6,30},{7,5},{8,0},{9,15},{... | collective-permute-start | bytes 995336 | tf_op jit(solution)/shard_map/cond/branch_1_fun/ppermute | solution.py:257
  13.8 5.1 %collective-permute-done = bf16[144,1152]{1,0:T(8,128)(2,1)S(1)} collective-permute-done((bf16[144,1152]{1,0:T(8,128)(2,1)S(1)}, bf16[144,1152]{1,0:T(8,128)(2,1)S(1)}, u32[]{:S(2)}, u32[]{:S(2)}) %collective-permute-start) | collective-permute-done | bytes 331808 | tf_op jit(solution)/shard_map/cond/branch_1_fun/ppermute | solution.py:257
  18.9 0.4 collective-permute-start.2
  19.3 0.9 %pad_maximum_fusion = bf16[2,144,1152]{2,1,0:T(8,128)(2,1)} fusion(bf16[1,144,1152]{2,1,0:T(8,128)(2,1)S(1)} %bitcast.10, bf16[1,144,1152]{2,1,0:T(8,128)(2,1)S(1)} %bitcast.8), kind=kLoop, calls=%fused_computation | loop fusion | flops 331776 | bytes 1327104 | tf_op jit(solution)/shard_map/cond/branch_1_fun/stack | solution.py:276
  20.2 1.6 %collective-permute-start.3 = (bf16[2,144,1152]{2,1,0:T(8,128)(2,1)}, bf16[2,144,1152]{2,1,0:T(8,128)(2,1)}, u32[]{:S(2)}, u32[]{:S(2)}) collective-permute-start(bf16[2,144,1152]{2,1,0:T(8,128)(2,1)} %pad_maximum_fusion), channel_id=1, source_target_pairs={{0,2},{1,9},{2,4},{3,11},{4,6},{5,13},{6,0},{7,15},{8,10},{9,17},{... | collective-permute-start | bytes 1990664 | tf_op jit(solution)/shard_map/cond/branch_1_fun/ppermute | solution.py:257
  21.8 0.5 collective-permute-start.6
  22.2 0.0 collective-permute-done.1
  22.2 8.5 %collective-permute-done.2 = bf16[144,1152]{1,0:T(8,128)(2,1)S(1)} collective-permute-done((bf16[144,1152]{1,0:T(8,128)(2,1)S(1)}, bf16[144,1152]{1,0:T(8,128)(2,1)S(1)}, u32[]{:S(2)}, u32[]{:S(2)}) %collective-permute-start.2) | collective-permute-done | bytes 331808 | tf_op jit(solution)/shard_map/cond/branch_1_fun/ppermute | solution.py:257
  30.7 0.9 %pad_maximum_fusion.1 = bf16[2,144,1152]{2,1,0:T(8,128)(2,1)} fusion(bf16[1,144,1152]{2,1,0:T(8,128)(2,1)S(1)} %bitcast.11, bf16[1,144,1152]{2,1,0:T(8,128)(2,1)S(1)} %bitcast.9), kind=kLoop, calls=%fused_computation.1 | loop fusion | flops 331776 | bytes 1327104 | tf_op jit(solution)/shard_map/cond/branch_1_fun/stack | solution.py:276
  31.6 0.0 collective-permute-start.4
  31.6 2.0 %collective-permute-start.5 = (bf16[2,144,1152]{2,1,0:T(8,128)(2,1)}, bf16[2,144,1152]{2,1,0:T(8,128)(2,1)}, u32[]{:S(2)}, u32[]{:S(2)}) collective-permute-start(bf16[2,144,1152]{2,1,0:T(8,128)(2,1)} %pad_maximum_fusion.1), channel_id=1, source_target_pairs={{0,2},{1,9},{2,4},{3,11},{4,6},{5,13},{6,0},{7,15},{8,10},{9,17},{... | collective-permute-start | bytes 1990664 | tf_op jit(solution)/shard_map/cond/branch_1_fun/ppermute | solution.py:257
  33.6 0.0 collective-permute-done.3
  33.6 0.2 collective-permute-start.10
  33.8 0.0 collective-permute-done.6
  33.8 2.6 %collective-permute-start.7 = (bf16[2,144,1152]{2,1,0:T(8,128)(2,1)}, bf16[2,144,1152]{2,1,0:T(8,128)(2,1)}, u32[]{:S(2)}, u32[]{:S(2)}) collective-permute-start(bf16[2,144,1152]{2,1,0:T(8,128)(2,1)} %collective-permute-done.3), channel_id=1, source_target_pairs={{0,2},{1,9},{2,4},{3,11},{4,6},{5,13},{6,0},{7,15},{8,10},{9,17},{... | collective-permute-start | bytes 1990664 | tf_op jit(solution)/shard_map/cond/branch_1_fun/ppermute | solution.py:257
  36.5 6.2 %collective-permute-done.4 = bf16[2,144,1152]{2,1,0:T(8,128)(2,1)} collective-permute-done((bf16[2,144,1152]{2,1,0:T(8,128)(2,1)}, bf16[2,144,1152]{2,1,0:T(8,128)(2,1)}, u32[]{:S(2)}, u32[]{:S(2)}) %collective-permute-start.4) | collective-permute-done | bytes 663584 | tf_op jit(solution)/shard_map/cond/branch_1_fun/ppermute | solution.py:257
  42.6 0.0 collective-permute-start.14
  42.6 0.5 collective-permute-start.12
  43.1 6.6 %collective-permute-done.7 = bf16[2,144,1152]{2,1,0:T(8,128)(2,1)} collective-permute-done((bf16[2,144,1152]{2,1,0:T(8,128)(2,1)}, bf16[2,144,1152]{2,1,0:T(8,128)(2,1)}, u32[]{:S(2)}, u32[]{:S(2)}) %collective-permute-start.7) | collective-permute-done | bytes 663584 | tf_op jit(solution)/shard_map/cond/branch_1_fun/ppermute | solution.py:257
  49.7 0.5 collective-permute-start.15
  50.2 4.1 %collective-permute-done.8 = bf16[2,144,1152]{2,1,0:T(8,128)(2,1)} collective-permute-done((bf16[2,144,1152]{2,1,0:T(8,128)(2,1)}, bf16[2,144,1152]{2,1,0:T(8,128)(2,1)}, u32[]{:S(2)}, u32[]{:S(2)}) %collective-permute-start.8) | collective-permute-done | bytes 663584 | tf_op jit(solution)/shard_map/cond/branch_1_fun/ppermute | solution.py:257
  54.3 2.4 %collective-permute-done.16 = bf16[2,144,1152]{2,1,0:T(8,128)(2,1)} collective-permute-done((bf16[2,144,1152]{2,1,0:T(8,128)(2,1)}, bf16[2,144,1152]{2,1,0:T(8,128)(2,1)}, u32[]{:S(2)}, u32[]{:S(2)}) %collective-permute-start.16) | collective-permute-done | bytes 663584 | tf_op jit(solution)/shard_map/cond/branch_1_fun/ppermute | solution.py:257
  56.8 3.8 %all-to-all-done.arrived = bf16[4,4,64,2304]{3,2,1,0:T(8,128)(2,1)} async-done(((bf16[4,4,64,2304]{3,2,1,0:T(8,128)(2,1)}), bf16[4,4,64,2304]{3,2,1,0:T(8,128)(2,1)}, u32[]{:S(2)}, u32[]{:S(2)}) %all-to-all-start) | async-done | bytes 4718624 | tf_op jit(solution)/shard_map/all_to_all | solution.py:292
  60.6 16.6 %shard_map.47 = bf16[16,64,2304]{2,1,0:T(8,128)(2,1)} custom-call(s32[8]{0:T(128)} %get-tuple-element.24.code, bf16[8,64,2304]{2,1,0:T(8,128)(2,1)} %local.1, bf16[4,4,64,2304]{3,2,1,0:T(8,128)(2,1)} %all-to-all-done.arrived, bf16[2,144,1152]{2,1,0:T(8,128)(2,1)} %get-tuple-element.26.refs_0_, bf16[2,144,1152]{2,1,0:T(8,128)(2,1)} %get-tuple-element.27.refs_1_, ...), custom_call_target="tpu_custom_call" | custom-call | flops 8833204224 | bytes 20000000 | tf_op jit(solution)/shard_map/pallas_call | solution.py:215
  (17 shorter events, 0.1 us)
Async XLA Ops:
  3.1 5.6 %copy-start = (bf16[72,2304]{1,0:T(8,128)(2,1)S(1)}, bf16[72,2304]{1,0:T(8,128)(2,1)}, u32[]{:S(2)}) copy-start(bf16[72,2304]{1,0:T(8,128)(2,1)} %param.9) | copy-start | bytes 995332
  3.1 5.6 %copy-start.1 = (s32[8,1]{0,1:T(1,128)S(1)}, s32[8,1]{0,1:T(1,128)}, u32[]{:S(2)}) copy-start(s32[8,1]{0,1:T(1,128)} %param.8) | copy-start | bytes 100
  3.2 57.4 %all-to-all-start = ((bf16[4,4,64,2304]{3,2,1,0:T(8,128)(2,1)}), bf16[4,4,64,2304]{3,2,1,0:T(8,128)(2,1)}, u32[]{:S(2)}, u32[]{:S(2)}) async-start(bf16[4,4,64,2304]{3,2,1,0:T(8,128)(2,1)} %get-tuple-element.25), calls=%async_computation | async-start | bytes 9437184 | tf_op jit(solution)/shard_map/all_to_all | solution.py:292
  8.7 1.6 %collective-permute-start.17 = (bf16[72,2304]{1,0:T(8,128)(2,1)S(1)}, bf16[72,2304]{1,0:T(8,128)(2,1)S(1)}, u32[]{:S(2)}, u32[]{:S(2)}) collective-permute-start(bf16[72,2304]{1,0:T(8,128)(2,1)S(1)} %copy-done), channel_id=1, source_target_pairs={{0,1},{1,0},{2,3},{3,2},{4,5},{5,4},{6,7},{7,6},{8,9},{9,8},{10,11... | collective-permute-start | bytes 995336 | tf_op jit(solution)/shard_map/ppermute | solution.py:257
  10.5 8.4 %collective-permute-start = (bf16[144,1152]{1,0:T(8,128)(2,1)S(1)}, bf16[144,1152]{1,0:T(8,128)(2,1)S(1)}, u32[]{:S(2)}, u32[]{:S(2)}) collective-permute-start(bf16[144,1152]{1,0:T(8,128)(2,1)S(1)} %param.1), channel_id=1, source_target_pairs={{0,8},{1,3},{2,10},{3,5},{4,12},{5,7},{6,14},{7,1},{8,16},{9,11},{... | collective-permute-start | bytes 995336 | tf_op jit(solution)/shard_map/cond/branch_1_fun/ppermute | solution.py:257
  12.2 10.1 %collective-permute-start.1 = (bf16[144,1152]{1,0:T(8,128)(2,1)S(1)}, bf16[144,1152]{1,0:T(8,128)(2,1)S(1)}, u32[]{:S(2)}, u32[]{:S(2)}) collective-permute-start(bf16[144,1152]{1,0:T(8,128)(2,1)S(1)} %param.1), channel_id=1, source_target_pairs={{0,24},{1,7},{2,26},{3,1},{4,28},{5,3},{6,30},{7,5},{8,0},{9,15},{... | collective-permute-start | bytes 995336 | tf_op jit(solution)/shard_map/cond/branch_1_fun/ppermute | solution.py:257
  18.9 11.8 %collective-permute-start.2 = (bf16[144,1152]{1,0:T(8,128)(2,1)S(1)}, bf16[144,1152]{1,0:T(8,128)(2,1)S(1)}, u32[]{:S(2)}, u32[]{:S(2)}) collective-permute-start(bf16[144,1152]{1,0:T(8,128)(2,1)S(1)} %collective-permute-done), channel_id=1, source_target_pairs={{0,8},{1,3},{2,10},{3,5},{4,12},{5,7},{6,14},{7,1},{8,16},{9,11},{... | collective-permute-start | bytes 995336 | tf_op jit(solution)/shard_map/cond/branch_1_fun/ppermute | solution.py:257
  20.2 13.4 %collective-permute-start.3 = (bf16[2,144,1152]{2,1,0:T(8,128)(2,1)}, bf16[2,144,1152]{2,1,0:T(8,128)(2,1)}, u32[]{:S(2)}, u32[]{:S(2)}) collective-permute-start(bf16[2,144,1152]{2,1,0:T(8,128)(2,1)} %pad_maximum_fusion), channel_id=1, source_target_pairs={{0,2},{1,9},{2,4},{3,11},{4,6},{5,13},{6,0},{7,15},{8,10},{9,17},{... | collective-permute-start | bytes 1990664 | tf_op jit(solution)/shard_map/cond/branch_1_fun/ppermute | solution.py:257
  21.8 12.1 %collective-permute-start.6 = (bf16[2,144,1152]{2,1,0:T(8,128)(2,1)}, bf16[2,144,1152]{2,1,0:T(8,128)(2,1)}, u32[]{:S(2)}, u32[]{:S(2)}) collective-permute-start(bf16[2,144,1152]{2,1,0:T(8,128)(2,1)} %pad_maximum_fusion), channel_id=1, source_target_pairs={{0,6},{1,25},{2,0},{3,27},{4,2},{5,29},{6,4},{7,31},{8,14},{9,1},{... | collective-permute-start | bytes 1990664 | tf_op jit(solution)/shard_map/cond/branch_1_fun/ppermute | solution.py:257
  22.2 14.2 %collective-permute-start.9 = (bf16[2,144,1152]{2,1,0:T(8,128)(2,1)}, bf16[2,144,1152]{2,1,0:T(8,128)(2,1)}, u32[]{:S(2)}, u32[]{:S(2)}) collective-permute-start(bf16[2,144,1152]{2,1,0:T(8,128)(2,1)} %pad_maximum_fusion), channel_id=1, source_target_pairs={{0,1},{1,0},{2,3},{3,2},{4,5},{5,4},{6,7},{7,6},{8,9},{9,8},{10,11... | collective-permute-start | bytes 1990664 | tf_op jit(solution)/shard_map/cond/branch_1_fun/ppermute | solution.py:257
  31.6 11.0 %collective-permute-start.4 = (bf16[2,144,1152]{2,1,0:T(8,128)(2,1)}, bf16[2,144,1152]{2,1,0:T(8,128)(2,1)}, u32[]{:S(2)}, u32[]{:S(2)}) collective-permute-start(bf16[2,144,1152]{2,1,0:T(8,128)(2,1)} %pad_maximum_fusion.1), channel_id=1, source_target_pairs={{0,6},{1,25},{2,0},{3,27},{4,2},{5,29},{6,4},{7,31},{8,14},{9,1},{... | collective-permute-start | bytes 1990664 | tf_op jit(solution)/shard_map/cond/branch_1_fun/ppermute | solution.py:257
  31.6 11.0 %collective-permute-start.5 = (bf16[2,144,1152]{2,1,0:T(8,128)(2,1)}, bf16[2,144,1152]{2,1,0:T(8,128)(2,1)}, u32[]{:S(2)}, u32[]{:S(2)}) collective-permute-start(bf16[2,144,1152]{2,1,0:T(8,128)(2,1)} %pad_maximum_fusion.1), channel_id=1, source_target_pairs={{0,2},{1,9},{2,4},{3,11},{4,6},{5,13},{6,0},{7,15},{8,10},{9,17},{... | collective-permute-start | bytes 1990664 | tf_op jit(solution)/shard_map/cond/branch_1_fun/ppermute | solution.py:257
  33.6 9.0 %collective-permute-start.10 = (bf16[2,144,1152]{2,1,0:T(8,128)(2,1)}, bf16[2,144,1152]{2,1,0:T(8,128)(2,1)}, u32[]{:S(2)}, u32[]{:S(2)}) collective-permute-start(bf16[2,144,1152]{2,1,0:T(8,128)(2,1)} %pad_maximum_fusion.1), channel_id=1, source_target_pairs={{0,1},{1,0},{2,3},{3,2},{4,5},{5,4},{6,7},{7,6},{8,9},{9,8},{10,11... | collective-permute-start | bytes 1990664 | tf_op jit(solution)/shard_map/cond/branch_1_fun/ppermute | solution.py:257
  33.8 15.9 %collective-permute-start.7 = (bf16[2,144,1152]{2,1,0:T(8,128)(2,1)}, bf16[2,144,1152]{2,1,0:T(8,128)(2,1)}, u32[]{:S(2)}, u32[]{:S(2)}) collective-permute-start(bf16[2,144,1152]{2,1,0:T(8,128)(2,1)} %collective-permute-done.3), channel_id=1, source_target_pairs={{0,2},{1,9},{2,4},{3,11},{4,6},{5,13},{6,0},{7,15},{8,10},{9,17},{... | collective-permute-start | bytes 1990664 | tf_op jit(solution)/shard_map/cond/branch_1_fun/ppermute | solution.py:257
  36.5 13.3 %collective-permute-start.11 = (bf16[2,144,1152]{2,1,0:T(8,128)(2,1)}, bf16[2,144,1152]{2,1,0:T(8,128)(2,1)}, u32[]{:S(2)}, u32[]{:S(2)}) collective-permute-start(bf16[2,144,1152]{2,1,0:T(8,128)(2,1)} %collective-permute-done.3), channel_id=1, source_target_pairs={{0,1},{1,0},{2,3},{3,2},{4,5},{5,4},{6,7},{7,6},{8,9},{9,8},{10,11... | collective-permute-start | bytes 1990664 | tf_op jit(solution)/shard_map/cond/branch_1_fun/ppermute | solution.py:257
  42.6 11.7 %collective-permute-start.8 = (bf16[2,144,1152]{2,1,0:T(8,128)(2,1)}, bf16[2,144,1152]{2,1,0:T(8,128)(2,1)}, u32[]{:S(2)}, u32[]{:S(2)}) collective-permute-start(bf16[2,144,1152]{2,1,0:T(8,128)(2,1)} %collective-permute-done.4), channel_id=1, source_target_pairs={{0,6},{1,25},{2,0},{3,27},{4,2},{5,29},{6,4},{7,31},{8,14},{9,1},{... | collective-permute-start | bytes 1990664 | tf_op jit(solution)/shard_map/cond/branch_1_fun/ppermute | solution.py:257
  42.6 11.7 %collective-permute-start.14 = (bf16[2,144,1152]{2,1,0:T(8,128)(2,1)}, bf16[2,144,1152]{2,1,0:T(8,128)(2,1)}, u32[]{:S(2)}, u32[]{:S(2)}) collective-permute-start(bf16[2,144,1152]{2,1,0:T(8,128)(2,1)} %collective-permute-done.6), channel_id=1, source_target_pairs={{0,1},{1,0},{2,3},{3,2},{4,5},{5,4},{6,7},{7,6},{8,9},{9,8},{10,11... | collective-permute-start | bytes 1990664 | tf_op jit(solution)/shard_map/cond/branch_1_fun/ppermute | solution.py:257
  42.6 11.7 %collective-permute-start.12 = (bf16[2,144,1152]{2,1,0:T(8,128)(2,1)}, bf16[2,144,1152]{2,1,0:T(8,128)(2,1)}, u32[]{:S(2)}, u32[]{:S(2)}) collective-permute-start(bf16[2,144,1152]{2,1,0:T(8,128)(2,1)} %collective-permute-done.4), channel_id=1, source_target_pairs={{0,1},{1,0},{2,3},{3,2},{4,5},{5,4},{6,7},{7,6},{8,9},{9,8},{10,11... | collective-permute-start | bytes 1990664 | tf_op jit(solution)/shard_map/cond/branch_1_fun/ppermute | solution.py:257
  49.7 4.6 %collective-permute-start.13 = (bf16[2,144,1152]{2,1,0:T(8,128)(2,1)}, bf16[2,144,1152]{2,1,0:T(8,128)(2,1)}, u32[]{:S(2)}, u32[]{:S(2)}) collective-permute-start(bf16[2,144,1152]{2,1,0:T(8,128)(2,1)} %collective-permute-done.5), channel_id=1, source_target_pairs={{0,1},{1,0},{2,3},{3,2},{4,5},{5,4},{6,7},{7,6},{8,9},{9,8},{10,11... | collective-permute-start | bytes 1990664 | tf_op jit(solution)/shard_map/cond/branch_1_fun/ppermute | solution.py:257
  49.7 4.6 %collective-permute-start.15 = (bf16[2,144,1152]{2,1,0:T(8,128)(2,1)}, bf16[2,144,1152]{2,1,0:T(8,128)(2,1)}, u32[]{:S(2)}, u32[]{:S(2)}) collective-permute-start(bf16[2,144,1152]{2,1,0:T(8,128)(2,1)} %collective-permute-done.7), channel_id=1, source_target_pairs={{0,1},{1,0},{2,3},{3,2},{4,5},{5,4},{6,7},{7,6},{8,9},{9,8},{10,11... | collective-permute-start | bytes 1990664 | tf_op jit(solution)/shard_map/cond/branch_1_fun/ppermute | solution.py:257
  54.3 2.5 %collective-permute-start.16 = (bf16[2,144,1152]{2,1,0:T(8,128)(2,1)}, bf16[2,144,1152]{2,1,0:T(8,128)(2,1)}, u32[]{:S(2)}, u32[]{:S(2)}) collective-permute-start(bf16[2,144,1152]{2,1,0:T(8,128)(2,1)} %collective-permute-done.8), channel_id=1, source_target_pairs={{0,1},{1,0},{2,3},{3,2},{4,5},{5,4},{6,7},{7,6},{8,9},{9,8},{10,11... | collective-permute-start | bytes 1990664 | tf_op jit(solution)/shard_map/cond/branch_1_fun/ppermute | solution.py:257
